TPU v7x, 1024 devices: a whole 4x8x16 slice. The times are simulated.
1024 devices in a mesh: section: 16 (over z), expert: 64 (over y, x, core).
Axes of the slice: x: 4, y: 8, z: 16, core: 2. Of those that a mesh axis runs over, the one named last changes fastest.
Arguments:
- carried: bfloat16 [16, 12288, 2048], P('section', 'expert'), may hold values from -6 to 6
- norm_gain: float32 [16, 2048], P('section'), may hold values from 0.25 to 1.75
- w_up: bfloat16 [16, 2048, 12288], P('section', None, 'expert'), may hold values from -0.125 to 0.125
- w_down: bfloat16 [16, 12288, 2048], P('section', 'expert'), may hold values from -0.21875 to 0.21875
- routes: int32 [1, 16, 12288, 2], P(None, 'section', 'expert'), may hold values from 0 to 15, all different within a row; in each aligned block of 192 rows (0 to 191, 192 to 383, ..., all dimensions but the last counted through in order) at most 32 rows name the same one
- gate_weights: float32 [1, 16, 12288, 2], P(None, 'section', 'expert'), may hold values from 0.3 to 1
Outputs:
- advanced: bfloat16 [16, 12288, 2048], P('section', 'expert')
Inputs may be any that keep to these rules, and one draw needn't show every extreme that they name: `routes`: each token names two different experts. Among the 192 tokens of one device at one step and section, no expert is named more than 32 times, a bound that some block reaches.
All inputs are finite; a program needn't handle non-finite values.
Results may differ from a plain program's by a relative error of at most 0.0052.
Values may be sent and summed in bfloat16 or wider, within the bound.
A program may use at most 32 MiB of HBM per device.

v0:
```python
import jax
import jax.numpy as jnp
from jax import lax
from jax.sharding import PartitionSpec as P


def partner(block, axis, distance):
    count = lax.axis_size(axis)
    route = []
    for low in range(count):
        high = low | 1 << distance
        if high != low and high < count:
            route += [(low, high), (high, low)]
    return lax.ppermute(block, axis, route)


def shifted(value, axis, steps):
    count = lax.axis_size(axis)
    pairs = [(source, (source + steps) % count) for source in range(count)]
    return lax.ppermute(value, axis, pairs)


def shards(carried, norm_gain, w_up, w_down, routes, gate_weights):
    devices = lax.axis_size("expert")
    experts = devices // 4
    tok_rows = carried.shape[1]
    model_width = carried.shape[2]
    capacity = min(tok_rows, 4 * ((5 * tok_rows + 8 * experts - 1) // (8 * experts)))
    quarter_cap = capacity // 4
    slot_count = devices * quarter_cap
    up_own = w_up[0]
    down_own = w_down[0]
    gain_row = norm_gain[0]
    up_stack = up_own[None]
    down_stack = down_own[None]
    for bit_index in range(2):
        got_up, got_down = partner((up_stack, down_stack), "expert", bit_index)
        up_stack = jnp.concatenate([up_stack, got_up], axis=0)
        down_stack = jnp.concatenate([down_stack, got_down], axis=0)
    quarter_width = up_own.shape[1]
    up_halves = up_stack.reshape(2, 2, model_width, quarter_width)
    down_halves = down_stack.reshape(2, 2, quarter_width, model_width)
    current = carried[0]
    expert_ids = routes[0, 0].reshape(-1)
    weights_now = gate_weights[0, 0]
    values = current.astype(jnp.float32)
    inverse_rms = lax.rsqrt(jnp.mean(values * values, axis=-1, keepdims=True) + 1e-05)
    normed = (values * inverse_rms * gain_row).astype(jnp.bfloat16)
    one_hot = (expert_ids[:, None] == jnp.arange(experts, dtype=jnp.int32)[None, :]).astype(
        jnp.int32
    )
    position = jnp.sum((jnp.cumsum(one_hot, axis=0) - one_hot) * one_hot, axis=1)
    target = (4 * expert_ids + position % 4) * quarter_cap + position // 4
    matches = target[:, None] == jnp.arange(slot_count, dtype=jnp.int32)[None, :]
    assign = (
        jnp.sum(matches.reshape(tok_rows, 2, slot_count).astype(jnp.int32), axis=1)
        .astype(jnp.bfloat16)
        .T
    )
    send_rows = jnp.dot(assign, normed, preferred_element_type=jnp.float32).astype(jnp.bfloat16)
    received = lax.all_to_all(
        send_rows.reshape(devices, quarter_cap, model_width),
        "expert",
        split_axis=0,
        concat_axis=0,
        tiled=True,
    )
    received = received.reshape(slot_count, model_width)
    hidden = jax.nn.gelu(
        jnp.einsum("sd,pqdh->pqsh", received, up_halves, preferred_element_type=jnp.float32)
    ).astype(jnp.bfloat16)
    parts = jnp.einsum(
        "pqsh,pqhd->psd", hidden, down_halves, preferred_element_type=jnp.float32
    ).astype(jnp.bfloat16)
    expert_rows = (parts[0].astype(jnp.float32) + parts[1].astype(jnp.float32)).astype(jnp.bfloat16)
    results = lax.all_to_all(
        expert_rows.reshape(devices, quarter_cap, model_width),
        "expert",
        split_axis=0,
        concat_axis=0,
        tiled=True,
    )
    results = results.reshape(slot_count, model_width)
    gathered = results[target].astype(jnp.float32).reshape(tok_rows, 2, model_width)
    updated = values + weights_now[:, 0:1] * gathered[:, 0] + weights_now[:, 1:2] * gathered[:, 1]
    current = shifted(updated.astype(jnp.bfloat16), "section", 1)
    return current[None]


def solution(mesh):
    in_specs = (
        P("section", "expert", None),
        P("section", None),
        P("section", None, "expert"),
        P("section", "expert", None),
        P(None, "section", "expert", None),
        P(None, "section", "expert", None),
    )
    out_specs = P("section", "expert", None)
    return jax.shard_map(shards, mesh=mesh, in_specs=in_specs, out_specs=out_specs, check_vma=False)
```

profile of v0, /device:TPU:1, one launch (start us, length us, event | category | flops | bytes accessed | tf_op | source)
XLA Modules:
  0.0 232.0 jit_solution(1431740637846919209)
XLA Ops:
  0.0 0.9 copy.16
  0.9 0.1 eq.45
  1.0 0.1 eq.41
  1.2 1.4 fusion.12
  2.6 0.9 reduce-window.6
  3.4 0.2 slice_reduce_fusion
  3.7 0.1 fusion.37
  3.8 0.1 reduce_sum.32
  3.9 0.1 fusion.30
  4.0 0.1 copy.20
  4.1 0.1 convert_reduce_fusion
  4.3 0.0 copy-done
  4.3 0.0 copy-done.6
  4.3 2.2 fusion
  6.5 19.2 %all-to-all-start = ((bf16[64,8,2048]{2,1,0:T(8,128)(2,1)}), bf16[64,8,2048]{2,1,0:T(8,128)(2,1)}, u32[]{:S(2)}, u32[]{:S(2)}) async-start(bf16[64,8,2048]{2,1,0:T(8,128)(2,1)} %fusion), calls=%async_computation | async-start | bytes 4194304 | tf_op jit(solution)/shard_map/all_to_all | solution.py:61
  25.7 0.0 copy-done.2
  25.7 2.5 %collective-permute-start = (bf16[1,2048,192]{1,2,0:T(8,128)(2,1)S(1)}, bf16[1,2048,192]{1,2,0:T(8,128)(2,1)S(1)}, u32[]{:S(2)}, u32[]{:S(2)}) collective-permute-start(bf16[1,2048,192]{1,2,0:T(8,128)(2,1)S(1)} %copy-done.2), channel_id=1, source_target_pairs={{0,1},{1,0},{2,3},{3,2},{4,5},{5,4},{6,7},{7,6},{8,9},{9,8},{10,11... | collective-permute-start | bytes 2359304 | tf_op jit(solution)/shard_map/ppermute | solution.py:14
  28.2 0.0 copy-done.4
  28.3 1.9 collective-permute-start.2
  30.2 0.0 collective-permute-done
  30.2 0.1 pad_maximum_fusion.2
  30.3 0.0 copy-start.3
  30.4 3.3 %collective-permute-start.1 = (bf16[2,2048,192]{1,2,0:T(8,128)(2,1)S(1)}, bf16[2,2048,192]{1,2,0:T(8,128)(2,1)S(1)}, u32[]{:S(2)}, u32[]{:S(2)}) collective-permute-start(bf16[2,2048,192]{1,2,0:T(8,128)(2,1)S(1)} %pad_maximum_fusion.2), channel_id=1, source_target_pairs={{0,2},{2,0},{1,3},{3,1},{4,6},{6,4},{5,7},{7,5},{8,10},{10,8},{9,1... | collective-permute-start | bytes 4718600 | tf_op jit(solution)/shard_map/ppermute | solution.py:14
  33.7 0.0 collective-permute-done.2
  33.7 0.1 pad_maximum_fusion.3
  33.8 0.0 copy-start.5
  33.8 2.3 collective-permute-start.3
  36.1 48.7 %collective-permute-done.1 = bf16[2,2048,192]{1,2,0:T(8,128)(2,1)S(1)} collective-permute-done((bf16[2,2048,192]{1,2,0:T(8,128)(2,1)S(1)}, bf16[2,2048,192]{1,2,0:T(8,128)(2,1)S(1)}, u32[]{:S(2)}, u32[]{:S(2)}) %collective-permute-start.1) | collective-permute-done | bytes 1572896 | tf_op jit(solution)/shard_map/ppermute | solution.py:14
  84.8 0.0 copy-done.3
  84.8 0.3 pad_maximum_fusion
  85.1 33.4 %collective-permute-done.3 = bf16[2,192,2048]{2,1,0:T(8,128)(2,1)S(1)} collective-permute-done((bf16[2,192,2048]{2,1,0:T(8,128)(2,1)S(1)}, bf16[2,192,2048]{2,1,0:T(8,128)(2,1)S(1)}, u32[]{:S(2)}, u32[]{:S(2)}) %collective-permute-start.3) | collective-permute-done | bytes 1572896 | tf_op jit(solution)/shard_map/ppermute | solution.py:14
  118.5 0.0 copy-done.5
  118.5 2.0 pad_maximum_fusion.1
  120.5 0.0 all-to-all-done
  120.5 8.7 %bitcast_convert_fusion = bf16[2,512,2048]{2,1,0:T(8,128)(2,1)} fusion(bf16[2,2,192,2048]{3,2,1,0:T(8,128)(2,1)} %bitcast.82, bf16[2,2,2048,192]{2,3,1,0:T(8,128)(2,1)S(1)} %bitcast.81, bf16[64,8,2048]{2,1,0:T(8,128)(2,1)} %all-to-all-done), kind=kOutput, calls=%fused_computation.1 | convolution fusion | flops 3226861568 | bytes 12582912 | tf_op jit(solution)/shard_map/pqsh,pqhd->psd/dot_general | solution.py:72
  129.2 4.5 %fusion.1 = bf16[64,8,2048]{2,1,0:T(8,128)(2,1)} fusion(bf16[2,512,2048]{2,1,0:T(8,128)(2,1)} %bitcast_convert_fusion), kind=kLoop, calls=%fused_computation.11 | loop fusion | flops 4194304 | bytes 6291456 | tf_op jit(solution)/shard_map/convert_element_type | solution.py:75
  133.7 10.8 %all-to-all-start.1 = ((bf16[64,8,2048]{2,1,0:T(8,128)(2,1)}), bf16[64,8,2048]{2,1,0:T(8,128)(2,1)S(1)}, u32[]{:S(2)}, u32[]{:S(2)}) async-start(bf16[64,8,2048]{2,1,0:T(8,128)(2,1)} %fusion.1), calls=%async_computation.1 | async-start | bytes 4194304 | tf_op jit(solution)/shard_map/all_to_all | solution.py:76
  144.5 0.1 mul.133
  144.7 0.0 copy-done.7
  144.7 49.4 %all-to-all-done.1 = bf16[64,8,2048]{2,1,0:T(8,128)(2,1)S(1)} async-done(((bf16[64,8,2048]{2,1,0:T(8,128)(2,1)}), bf16[64,8,2048]{2,1,0:T(8,128)(2,1)S(1)}, u32[]{:S(2)}, u32[]{:S(2)}) %all-to-all-start.1) | async-done | bytes 2097184 | tf_op jit(solution)/shard_map/all_to_all | solution.py:76
  194.1 3.1 %gather_fusion = bf16[384,2048]{1,0:T(8,128)(2,1)} fusion(bf16[512,2048]{1,0:T(8,128)(2,1)S(1)} %bitcast.80, s32[1024]{0:T(1024)S(1)} %pad_clamp_fusion), kind=kCustom, calls=%fused_computation | custom fusion | bytes 3147264 | tf_op jit(solution)/shard_map/gather | solution.py:84
  197.3 3.4 %reshape.175 = f32[192,2,2048]{2,1,0:T(2,128)S(1)} reshape(bf16[384,2048]{1,0:T(8,128)(2,1)} %gather_fusion) | data formatting | bytes 4718592 | tf_op jit(solution)/shard_map/convert_element_type | solution.py:84
  200.7 0.0 copy-start.1
  200.7 2.4 %fusion.45 = (f32[192,1,2048]{2,1,0:T(1,128)S(1)}, f32[192,1,2048]{2,1,0:T(1,128)S(1)}) fusion(f32[192,2,2048]{2,1,0:T(2,128)S(1)} %reshape.175), kind=kLoop, calls=%fused_computation.76 | loop fusion | bytes 6291456 | tf_op jit(solution)/shard_map/slice | solution.py:85
  203.1 1.7 fusion.16
  204.8 1.9 collective-permute-start.4
  206.8 24.3 %collective-permute-done.4 = bf16[192,2048]{1,0:T(8,128)(2,1)S(1)} collective-permute-done((bf16[192,2048]{1,0:T(8,128)(2,1)S(1)}, bf16[192,2048]{1,0:T(8,128)(2,1)S(1)}, u32[]{:S(2)}, u32[]{:S(2)}) %collective-permute-start.4) | collective-permute-done | bytes 786464 | tf_op jit(solution)/shard_map/ppermute | solution.py:20
  231.1 0.9 copy.40
  (13 shorter events, 0.1 us)
Async XLA Ops:
  0.0 4.3 %copy-start = (bf16[1,192,2048]{2,1,0:T(8,128)(2,1)S(1)}, bf16[1,192,2048]{2,1,0:T(8,128)(2,1)}, u32[]{:S(2)}) copy-start(bf16[1,192,2048]{2,1,0:T(8,128)(2,1)} %param.6) | copy-start | bytes 2359300
  0.0 4.3 %copy-start.6 = (f32[1,2048]{1,0:T(1,128)S(1)}, f32[1,2048]{1,0:T(1,128)}, u32[]{:S(2)}) copy-start(f32[1,2048]{1,0:T(1,128)} %param.7) | copy-start | bytes 24580
  6.5 19.2 %copy-start.2 = (bf16[1,2048,192]{1,2,0:T(8,128)(2,1)S(1)}, bf16[1,2048,192]{1,2,0:T(8,128)(2,1)}, u32[]{:S(2)}) copy-start(bf16[1,2048,192]{1,2,0:T(8,128)(2,1)} %param.8) | copy-start | bytes 2359300
  6.5 21.8 %copy-start.4 = (bf16[1,192,2048]{2,1,0:T(8,128)(2,1)S(1)}, bf16[1,192,2048]{2,1,0:T(8,128)(2,1)}, u32[]{:S(2)}) copy-start(bf16[1,192,2048]{2,1,0:T(8,128)(2,1)} %param.9) | copy-start | bytes 2359300
  6.5 114.1 %all-to-all-start = ((bf16[64,8,2048]{2,1,0:T(8,128)(2,1)}), bf16[64,8,2048]{2,1,0:T(8,128)(2,1)}, u32[]{:S(2)}, u32[]{:S(2)}) async-start(bf16[64,8,2048]{2,1,0:T(8,128)(2,1)} %fusion), calls=%async_computation | async-start | bytes 4194304 | tf_op jit(solution)/shard_map/all_to_all | solution.py:61
  25.7 4.5 %collective-permute-start = (bf16[1,2048,192]{1,2,0:T(8,128)(2,1)S(1)}, bf16[1,2048,192]{1,2,0:T(8,128)(2,1)S(1)}, u32[]{:S(2)}, u32[]{:S(2)}) collective-permute-start(bf16[1,2048,192]{1,2,0:T(8,128)(2,1)S(1)} %copy-done.2), channel_id=1, source_target_pairs={{0,1},{1,0},{2,3},{3,2},{4,5},{5,4},{6,7},{7,6},{8,9},{9,8},{10,11... | collective-permute-start | bytes 2359304 | tf_op jit(solution)/shard_map/ppermute | solution.py:14
  28.3 5.4 %collective-permute-start.2 = (bf16[1,192,2048]{2,1,0:T(8,128)(2,1)S(1)}, bf16[1,192,2048]{2,1,0:T(8,128)(2,1)S(1)}, u32[]{:S(2)}, u32[]{:S(2)}) collective-permute-start(bf16[1,192,2048]{2,1,0:T(8,128)(2,1)S(1)} %copy-done.4), channel_id=1, source_target_pairs={{0,1},{1,0},{2,3},{3,2},{4,5},{5,4},{6,7},{7,6},{8,9},{9,8},{10,11... | collective-permute-start | bytes 2359304 | tf_op jit(solution)/shard_map/ppermute | solution.py:14
  30.3 54.5 %copy-start.3 = (bf16[1,2048,192]{1,2,0:T(8,128)(2,1)S(1)}, bf16[1,2048,192]{1,2,0:T(8,128)(2,1)}, u32[]{:S(2)}) copy-start(bf16[1,2048,192]{1,2,0:T(8,128)(2,1)} %param.8) | copy-start | bytes 2359300
  30.4 54.5 %collective-permute-start.1 = (bf16[2,2048,192]{1,2,0:T(8,128)(2,1)S(1)}, bf16[2,2048,192]{1,2,0:T(8,128)(2,1)S(1)}, u32[]{:S(2)}, u32[]{:S(2)}) collective-permute-start(bf16[2,2048,192]{1,2,0:T(8,128)(2,1)S(1)} %pad_maximum_fusion.2), channel_id=1, source_target_pairs={{0,2},{2,0},{1,3},{3,1},{4,6},{6,4},{5,7},{7,5},{8,10},{10,8},{9,1... | collective-permute-start | bytes 4718600 | tf_op jit(solution)/shard_map/ppermute | solution.py:14
  33.8 84.7 %copy-start.5 = (bf16[1,192,2048]{2,1,0:T(8,128)(2,1)S(1)}, bf16[1,192,2048]{2,1,0:T(8,128)(2,1)}, u32[]{:S(2)}) copy-start(bf16[1,192,2048]{2,1,0:T(8,128)(2,1)} %param.9) | copy-start | bytes 2359300
  33.8 84.7 %collective-permute-start.3 = (bf16[2,192,2048]{2,1,0:T(8,128)(2,1)S(1)}, bf16[2,192,2048]{2,1,0:T(8,128)(2,1)S(1)}, u32[]{:S(2)}, u32[]{:S(2)}) collective-permute-start(bf16[2,192,2048]{2,1,0:T(8,128)(2,1)S(1)} %pad_maximum_fusion.3), channel_id=1, source_target_pairs={{0,2},{2,0},{1,3},{3,1},{4,6},{6,4},{5,7},{7,5},{8,10},{10,8},{9,1... | collective-permute-start | bytes 4718600 | tf_op jit(solution)/shard_map/ppermute | solution.py:14
  133.7 11.0 %copy-start.7 = (f32[1,1,192,2]{2,3,1,0:T(2,128)S(1)}, f32[1,1,192,2]{2,3,1,0:T(2,128)}, u32[]{:S(2)}) copy-start(f32[1,1,192,2]{2,3,1,0:T(2,128)} %param.11) | copy-start | bytes 4612
  133.7 60.5 %all-to-all-start.1 = ((bf16[64,8,2048]{2,1,0:T(8,128)(2,1)}), bf16[64,8,2048]{2,1,0:T(8,128)(2,1)S(1)}, u32[]{:S(2)}, u32[]{:S(2)}) async-start(bf16[64,8,2048]{2,1,0:T(8,128)(2,1)} %fusion.1), calls=%async_computation.1 | async-start | bytes 4194304 | tf_op jit(solution)/shard_map/all_to_all | solution.py:76
  200.7 2.5 %copy-start.1 = (bf16[1,192,2048]{2,1,0:T(8,128)(2,1)S(1)}, bf16[1,192,2048]{2,1,0:T(8,128)(2,1)}, u32[]{:S(2)}) copy-start(bf16[1,192,2048]{2,1,0:T(8,128)(2,1)} %param.6) | copy-start | bytes 2359300
  204.8 26.3 %collective-permute-start.4 = (bf16[192,2048]{1,0:T(8,128)(2,1)S(1)}, bf16[192,2048]{1,0:T(8,128)(2,1)S(1)}, u32[]{:S(2)}, u32[]{:S(2)}) collective-permute-start(bf16[192,2048]{1,0:T(8,128)(2,1)S(1)} %fusion.16), channel_id=1, source_target_pairs={{0,64},{64,128},{128,192},{192,256},{256,320},{320,384},{384,448},... | collective-permute-start | bytes 2359304 | tf_op jit(solution)/shard_map/ppermute | solution.py:20
where the time goes:
time: 235 us; the launch traced here: 232 us
  waiting for transfers between devices  156 us (66%)
  starting transfers between devices  41.9 us (18%)
  local copies, waits for them, and re-layouts  11.6 us (5%)
  other arithmetic  11.4 us (5%)
  matrix products  10.9 us (5%)
    ppermute x4, waiting for transfers between devices, partner(): return lax.ppermute(block, axis, route)  82.1 us
    all_to_all x1, waiting for transfers between devices, shards(): lax.all_to_all(expert_rows.reshape(devices, quarter_cap, model_width), 'e...  49.4 us
    ppermute x1, waiting for transfers between devices, shifted(): return lax.ppermute(value, axis, pairs)  24.3 us
    all_to_all x1, starting transfers between devices, shards(): lax.all_to_all(send_rows.reshape(devices, quarter_cap, model_width), 'exp...  19.2 us
    all_to_all x1, starting transfers between devices, shards(): lax.all_to_all(expert_rows.reshape(devices, quarter_cap, model_width), 'e...  10.8 us
    ppermute x4, starting transfers between devices, partner(): return lax.ppermute(block, axis, route)  10 us
    dot_general x1, matrix products, shards(): jnp.einsum('pqsh,pqhd->psd', hidden, down_halves, preferred_element_type=...  8.68 us
  transfers between devices with their start and end apart: 7, of which 4 were waited for; matrix products, arithmetic and copies ran while one was open for 1% of the time, Pallas kernels for 0%

commit v1 on v0

v1 whole, which is shorter than its diff:
```python
import jax
import jax.numpy as jnp
from jax import lax
from jax.experimental import pallas as pl
from jax.experimental.pallas import tpu as pltpu
from jax.sharding import PartitionSpec as P

MESH = pl.DeviceIdType.MESH
NX, NY, NC = 4, 8, 2
CHIPS = NX * NY
ROWS = 16
CHUNKS = 4


def kernel(
    x_ref, gain_ref, up_ref, down_ref, routes_ref, gates_ref, out_ref,
    up_all, down_all, normed, send, recv, hidden, res, back, mix, outb,
    own_sem, sib_send, sib_recv, xp_send, xp_recv, fwd_send, fwd_recv,
    self_sem, go_send, go_recv, home_self, home_send, home_recv, out_send, out_recv,
):
    tokens, width = x_ref.shape
    quarter = up_ref.shape[0]
    slots = CHIPS * ROWS
    experts = CHIPS // 2
    cap = 2 * ROWS
    cols = width // CHUNKS
    sections = lax.axis_size("section")
    section = lax.axis_index("section")
    me = lax.axis_index("expert")
    core = lax.rem(me, NC)
    chip = lax.div(me, NC)
    x = lax.rem(chip, NX)
    y = lax.div(chip, NX)

    def away(i, sign):
        k, m = lax.div(i, NX), lax.rem(i, NX)
        dy = NY // 2 + (1 - 2 * lax.rem(k, 2)) * lax.div(k + 1, 2)
        dx = NX // 2 + (1 - 2 * lax.rem(m, 2)) * lax.div(m + 1, 2)
        return lax.rem(y + NY + sign * dy, NY) * NX + lax.rem(x + NX + sign * dx, NX)

    def at(which):
        return (section, which * NC + core)

    sibling = (section, chip * NC + 1 - core)
    beside = (section, (chip + 1 - 2 * lax.rem(x, 2)) * NC + core)
    following = (lax.rem(section + 1, sections), me)
    previous = (lax.rem(section + sections - 1, sections), me)

    barrier = pltpu.get_barrier_semaphore()

    def greet(i, carry):
        pl.semaphore_signal(barrier, inc=1, device_id=at(away(i, 1)), device_id_type=MESH)
        return carry

    lax.fori_loop(0, CHIPS - 1, greet, 0)
    pl.semaphore_signal(barrier, inc=1, device_id=sibling, device_id_type=MESH)
    pl.semaphore_signal(barrier, inc=1, device_id=previous, device_id_type=MESH)

    own_up = pltpu.make_async_copy(up_ref, up_all.at[pl.ds(0, quarter)], own_sem.at[0])
    own_down = pltpu.make_async_copy(down_ref, down_all.at[pl.ds(0, quarter)], own_sem.at[1])
    own_up.start()
    own_down.start()

    block = 48

    def norm(i, carry):
        rows = pl.ds(pl.multiple_of(i * block, 16), block)
        values = x_ref[rows, :].astype(jnp.float32)
        inverse = lax.rsqrt(jnp.mean(values * values, axis=-1, keepdims=True) + 1e-05)
        normed[rows, :] = (values * inverse * gain_ref[...]).astype(jnp.bfloat16)
        return carry

    lax.fori_loop(0, tokens // block, norm, 0)
    pl.semaphore_wait(barrier, CHIPS + 1)

    def remote(src, dst, send_sem, recv_sem, device):
        return pltpu.make_async_remote_copy(
            src_ref=src, dst_ref=dst, send_sem=send_sem, recv_sem=recv_sem,
            device_id=device, device_id_type=MESH,
        )

    beside_copies = [
        remote(own, whole.at[pl.ds(2 * quarter, quarter)], xp_send.at[j], xp_recv.at[j], beside)
        for j, (own, whole) in enumerate(((up_ref, up_all), (down_ref, down_all)))
    ]
    sibling_copies = [
        remote(own, whole.at[pl.ds(quarter, quarter)], sib_send.at[j], sib_recv.at[j], sibling)
        for j, (own, whole) in enumerate(((up_ref, up_all), (down_ref, down_all)))
    ]
    for copy in beside_copies + sibling_copies:
        copy.start()

    ids = routes_ref[...]
    names = lax.broadcasted_iota(jnp.int32, (experts, tokens), 0)
    first = (names == ids[0:1, :]).astype(jnp.float32)
    second = (names == ids[1:2, :]).astype(jnp.float32)
    earlier = (
        lax.broadcasted_iota(jnp.int32, (tokens, tokens), 0)
        < lax.broadcasted_iota(jnp.int32, (tokens, tokens), 1)
    ).astype(jnp.bfloat16)
    count = jnp.dot((first + second).astype(jnp.bfloat16), earlier, preferred_element_type=jnp.float32)
    place0 = jnp.sum(count * first, axis=0, keepdims=True).astype(jnp.int32) + ids[0:1, :] * cap
    place1 = jnp.sum(count * second, axis=0, keepdims=True).astype(jnp.int32) + ids[1:2, :] * cap
    slot = lax.broadcasted_iota(jnp.int32, (slots, tokens), 0)
    is0, is1 = slot == place0, slot == place1
    assign = (is0 | is1).astype(jnp.float32).astype(jnp.bfloat16)

    def fill(i, carry):
        part = pl.ds(pl.multiple_of(i * cols, 128), cols)
        send[:, part] = jnp.dot(
            assign, normed[:, part], preferred_element_type=jnp.float32
        ).astype(jnp.bfloat16)
        return carry

    lax.fori_loop(0, CHUNKS, fill, 0)

    def slots_of(which):
        return pl.ds(pl.multiple_of(which * ROWS, ROWS), ROWS)

    def go(i, carry):
        target = away(i, 1)
        remote(send.at[slots_of(target)], recv.at[slots_of(i)], go_send, go_recv, at(target)).start()
        return carry

    lax.fori_loop(0, CHIPS - 1, go, 0)
    stay = pltpu.make_async_copy(send.at[slots_of(chip)], recv.at[slots_of(CHIPS - 1)], self_sem)
    stay.start()

    gates = gates_ref[...]
    weight = jnp.where(is0, gates[0:1, :], 0.0) + jnp.where(is1, gates[1:2, :], 0.0)
    weight = weight.T
    high = weight.astype(jnp.bfloat16)
    mix[:, pl.ds(0, slots)] = high
    mix[:, pl.ds(slots, slots)] = (weight - high.astype(jnp.float32)).astype(jnp.bfloat16)

    forward_copies = [
        remote(
            whole.at[pl.ds(2 * quarter, quarter)], whole.at[pl.ds(3 * quarter, quarter)],
            fwd_send.at[j], fwd_recv.at[j], sibling,
        )
        for j, whole in enumerate((up_all, down_all))
    ]
    for j in range(2):
        beside_copies[j].wait_recv()
        forward_copies[j].start()
    own_up.wait()
    own_down.wait()
    for j in range(2):
        sibling_copies[j].wait()
    forward_copies[0].wait_recv()
    stay.wait()
    everyone = pl.ds(0, slots - ROWS)
    went = remote(send.at[everyone], recv.at[everyone], go_send, go_recv, sibling)
    went.wait_recv()

    units = 256

    def up(i, carry):
        part = pl.ds(pl.multiple_of(i * units, units), units)
        v = lax.dot_general(
            recv[...], up_all[part, :], (((1,), (1,)), ((), ())), preferred_element_type=jnp.float32
        )
        inner = 0.7978845608028654 * (v + 0.044715 * (v * v * v))
        hidden[:, part] = (0.5 * v * (1.0 + jnp.tanh(inner))).astype(jnp.bfloat16)
        return carry

    lax.fori_loop(0, 4 * quarter // units, up, 0)
    forward_copies[1].wait_recv()

    def down(c, carry):
        part = pl.ds(pl.multiple_of(c * cols, 128), cols)
        res[c] = jnp.dot(
            hidden[...], down_all[:, part], preferred_element_type=jnp.float32
        ).astype(jnp.bfloat16)

        def home(i, inner):
            target = away(i, -1)
            remote(
                res.at[c, slots_of(i)], back.at[c, slots_of(chip)],
                home_send.at[c], home_recv.at[c], at(target),
            ).start()
            return inner

        lax.fori_loop(0, CHIPS - 1, home, 0)
        pltpu.make_async_copy(
            res.at[c, slots_of(CHIPS - 1)], back.at[c, slots_of(chip)], home_self.at[c]
        ).start()
        return carry

    lax.fori_loop(0, CHUNKS, down, 0)

    def onward(c):
        part = pl.ds(pl.multiple_of(c * cols, 128), cols)
        return remote(outb.at[c], out_ref.at[:, part], out_send.at[c], out_recv.at[c], following)

    def came_home(c):
        return remote(res.at[c, everyone], back.at[c, everyone], home_send.at[c], home_recv.at[c], sibling)

    def finish(c, carry):
        part = pl.ds(pl.multiple_of(c * cols, 128), cols)
        pltpu.make_async_copy(
            res.at[c, slots_of(CHIPS - 1)], back.at[c, slots_of(chip)], home_self.at[c]
        ).wait()
        came_home(c).wait_recv()
        rows = back[c]
        total = jnp.dot(mix[:, pl.ds(0, slots)], rows, preferred_element_type=jnp.float32)
        total += jnp.dot(mix[:, pl.ds(slots, slots)], rows, preferred_element_type=jnp.float32)
        outb[c] = (x_ref[:, part].astype(jnp.float32) + total).astype(jnp.bfloat16)
        onward(c).start()
        return carry

    lax.fori_loop(0, CHUNKS, finish, 0)

    for j in range(2):
        beside_copies[j].wait_send()
        forward_copies[j].wait_send()
    went.wait_send()

    def drain(c, carry):
        came_home(c).wait_send()
        onward(c).wait()
        return carry

    lax.fori_loop(0, CHUNKS, drain, 0)


def shards(carried, norm_gain, w_up, w_down, routes, gate_weights):
    tokens, width = carried.shape[1:]
    quarter = w_down.shape[1]
    slots = CHIPS * ROWS
    cols = width // CHUNKS
    bf16 = jnp.bfloat16
    dma = pltpu.SemaphoreType.DMA
    vmem = pl.BlockSpec(memory_space=pltpu.VMEM)
    whole = pl.BlockSpec(memory_space=pl.ANY)
    out = pl.pallas_call(
        kernel,
        name="section_layer",
        out_shape=jax.ShapeDtypeStruct((tokens, width), bf16),
        in_specs=[vmem, vmem, whole, whole, vmem, vmem],
        out_specs=whole,
        scratch_shapes=[
            pltpu.VMEM((4 * quarter, width), bf16),
            pltpu.VMEM((4 * quarter, width), bf16),
            pltpu.VMEM((tokens, width), bf16),
            pltpu.VMEM((slots, width), bf16),
            pltpu.VMEM((slots, width), bf16),
            pltpu.VMEM((slots, 4 * quarter), bf16),
            pltpu.VMEM((CHUNKS, slots, cols), bf16),
            pltpu.VMEM((CHUNKS, slots, cols), bf16),
            pltpu.VMEM((tokens, 2 * slots), bf16),
            pltpu.VMEM((CHUNKS, tokens, cols), bf16),
            dma((2,)), dma((2,)), dma((2,)), dma((2,)), dma((2,)), dma((2,)), dma((2,)),
            dma, dma, dma,
            dma((CHUNKS,)), dma((CHUNKS,)), dma((CHUNKS,)), dma((CHUNKS,)), dma((CHUNKS,)),
        ],
        compiler_params=pltpu.CompilerParams(
            collective_id=0, has_side_effects=True, vmem_limit_bytes=52 * 1024 * 1024
        ),
        cost_estimate=pl.CostEstimate(
            flops=8 * slots * width * quarter * 2, bytes_accessed=4 * quarter * width * 2, transcendentals=0
        ),
    )(carried[0], norm_gain, w_up[0].T, w_down[0], routes[0, 0].T, gate_weights[0, 0].T)
    return out[None]


def solution(mesh):
    in_specs = (
        P("section", "expert", None),
        P("section", None),
        P("section", None, "expert"),
        P("section", "expert", None),
        P(None, "section", "expert", None),
        P(None, "section", "expert", None),
    )
    return jax.shard_map(
        shards, mesh=mesh, in_specs=in_specs, out_specs=P("section", "expert", None), check_vma=False
    )
```

time: 235 us -> 141 us (0.60)
  waiting for transfers between devices: 156 us -> 0 us
  Pallas kernels: 0 us -> 135 us
  starting transfers between devices: 41.9 us -> 0 us
  other arithmetic: 11.4 us -> 0 us
  matrix products: 10.9 us -> 0 us
  local copies, waits for them, and re-layouts: 11.6 us -> 4.07 us
    pallas_call x0 -> x1, Pallas kernels: none -> 135 us  [shards(): pl.pallas_call(kernel, name='section_layer', out_shape=jax.ShapeDtypeStru...]
    ppermute x5 -> x0, waiting for transfers between devices: 106 us -> none  [the longest x4 82.1 us: partner(): return lax.ppermute(block, axis, route)]
    all_to_all x2 -> x0, waiting for transfers between devices: 49.4 us -> none  [the longest x1 49.4 us: shards(): lax.all_to_all(expert_rows.reshape(devices, quarter_cap, model_width), 'e...]
    all_to_all x2 -> x0, starting transfers between devices: 30 us -> none  [the longest x1 19.2 us: shards(): lax.all_to_all(send_rows.reshape(devices, quarter_cap, model_width), 'exp...]
    ppermute x5 -> x0, starting transfers between devices: 11.9 us -> none  [the longest x4 10 us: partner(): return lax.ppermute(block, axis, route)]
    dot_general x2 -> x0, matrix products: 10.9 us -> none  [the longest x1 8.68 us: shards(): jnp.einsum('pqsh,pqhd->psd', hidden, down_halves, preferred_element_type=...]
    convert_element_type x3 -> x0, other arithmetic: 6.15 us -> none  [the longest x1 4.45 us: shards(): (parts[0].astype(jnp.float32) + parts[1].astype(jnp.float32)).astype(jnp....]
    convert_element_type x1 -> x0, local copies, waits for them, and re-layouts: 3.4 us -> none  [shards(): results[target].astype(jnp.float32).reshape(tok_rows, 2, model_width)]
  transfers between devices with their start and end apart: 7 -> 0, of which waited for: 4 -> 0; matrix products, arithmetic and copies ran while one was open for 1% -> 0% of each run, Pallas kernels for 0% -> 0%
where the time goes in v1:
time: 141 us; the launch traced here: 139 us
  Pallas kernels  135 us (96%)
  local copies, waits for them, and re-layouts  4.07 us (3%)
    pallas_call x1, Pallas kernels, shards(): pl.pallas_call(kernel, name='section_layer', out_shape=jax.ShapeDtypeStru...  135 us
    unnamed x9, local copies, waits for them, and re-layouts  4.07 us

profile of v1, /device:TPU:1, one launch (start us, length us, event | category | flops | bytes accessed | tf_op | source)
XLA Modules:
  0.0 139.3 jit_solution(13598977053420186043)
XLA Ops:
  0.0 0.0 copy-start.1
  0.0 0.7 copy-done.1
  0.7 0.0 copy-start
  0.7 1.1 copy-done
  1.8 0.0 copy-start.2
  1.8 0.7 copy-done.2
  2.5 0.0 copy-start.3
  2.5 0.7 copy-done.3
  3.2 135.2 %section_layer.1 = bf16[192,2048]{1,0:T(8,128)(2,1)S(1)} custom-call(bf16[192,2048]{1,0:T(8,128)(2,1)S(1)} %bitcast.13, f32[1,2048]{1,0:T(1,128)S(1)} %copy-done.1, bf16[192,2048]{1,0:T(8,128)(2,1)} %bitcast.16, bf16[192,2048]{1,0:T(8,128)(2,1)} %bitcast.17, s32[2,192]{1,0:T(2,128)S(1)} %bitcast.14, f32[2,192]{1,0:T(2,128)S(1)} %bitcast.15), custom_call_target="tpu_custom_call" | custom-call | flops 3221225472 | bytes 3145728 | tf_op jit(solution)/shard_map/section_layer/pallas_call | solution.py:236
  138.5 0.9 copy.8
Async XLA Ops:
  0.0 0.7 copy-start.1
  0.7 1.1 copy-start
  1.8 0.7 copy-start.2
  2.5 0.7 copy-start.3

commit v2 on v1

v2 whole, which is shorter than its diff:
```python
import jax
import jax.numpy as jnp
from jax import lax
from jax.experimental import pallas as pl
from jax.experimental.pallas import tpu as pltpu
from jax.sharding import PartitionSpec as P

MESH = pl.DeviceIdType.MESH
NX, NY, NC = 4, 8, 2
PEERS = 2 * NY
EXPERTS = NX * NY // 2
GROUPS = ((0, 10), (10, 16))
WIDTHS = (640, 640, 512, 256)
STARTS = tuple(sum(WIDTHS[:c]) for c in range(len(WIDTHS)))


def kernel(
    x_hbm, gain_hbm, up_ref, down_ref, routes_hbm, gates_hbm, out_ref,
    x_ref, gain_ref, routes_ref, gates_ref,
    up_all, down_all, normed, send, recv, hidden, mix, *rest,
):
    chunks = len(WIDTHS)
    res, back, outb = rest[:chunks], rest[chunks : 2 * chunks], rest[2 * chunks : 3 * chunks]
    (
        in_sem, own_sem, sib_send, sib_recv, xp_send, xp_recv, fwd_send, fwd_recv,
        self_sem, go_send, go_recv, home_self, home_send, home_recv, out_send, out_recv,
    ) = rest[3 * chunks :]
    tokens, width = x_ref.shape
    quarter = up_ref.shape[0]
    slots = send.shape[0]
    cap = slots // EXPERTS
    sections = lax.axis_size("section")
    section = lax.axis_index("section")
    me = lax.axis_index("expert")
    core = lax.rem(me, NC)
    chip = lax.div(me, NC)
    x = lax.rem(chip, NX)
    y = lax.div(chip, NX)
    mine = y * 2 + lax.div(x, 2)

    def peer(i, sign):
        k = lax.div(i, 2)
        half = lax.div(k + 1, 2)
        dy = half * (2 * lax.rem(k, 2) - 1)
        return lax.rem(y + NY + sign * dy, NY), lax.rem(i, 2) * (NX - 1 - 2 * x) + x

    def device(py, px):
        return (section, (py * NX + px) * NC + core)

    sibling = (section, chip * NC + 1 - core)
    beside = (section, (chip + 1 - 2 * lax.rem(x, 2)) * NC + core)
    following = (lax.rem(section + 1, sections), me)
    previous = (lax.rem(section + sections - 1, sections), me)

    def hello(target):
        pl.semaphore_signal(barrier, inc=1, device_id=target, device_id_type=MESH)

    barrier = pltpu.get_barrier_semaphore()
    inputs = [
        pltpu.make_async_copy(src, dst, in_sem.at[j])
        for j, (src, dst) in enumerate(
            ((routes_hbm, routes_ref), (gain_hbm, gain_ref), (x_hbm, x_ref), (gates_hbm, gates_ref))
        )
    ]
    for copy in inputs:
        copy.start()

    def greet(i, carry):
        hello(device(*peer(i, -1)))
        return carry

    lax.fori_loop(1, PEERS, greet, 0)
    hello(sibling)
    hello(beside)
    hello(previous)

    own = [
        pltpu.make_async_copy(src, dst.at[pl.ds(0, quarter)], own_sem.at[j])
        for j, (src, dst) in enumerate(((up_ref, up_all), (down_ref, down_all)))
    ]
    for copy in own:
        copy.start()

    inputs[0].wait()
    ids = routes_ref[...]
    names = lax.broadcasted_iota(jnp.int32, (EXPERTS, tokens), 0)
    first = (names == ids[0:1, :]).astype(jnp.float32)
    second = (names == ids[1:2, :]).astype(jnp.float32)
    earlier = (
        lax.broadcasted_iota(jnp.int32, (tokens, tokens), 0)
        < lax.broadcasted_iota(jnp.int32, (tokens, tokens), 1)
    ).astype(jnp.bfloat16)
    count = jnp.dot((first + second).astype(jnp.bfloat16), earlier, preferred_element_type=jnp.float32)
    place0 = jnp.sum(count * first, axis=0, keepdims=True).astype(jnp.int32) + ids[0:1, :] * cap
    place1 = jnp.sum(count * second, axis=0, keepdims=True).astype(jnp.int32) + ids[1:2, :] * cap
    slot = lax.broadcasted_iota(jnp.int32, (slots, tokens), 0)
    is0, is1 = slot == place0, slot == place1
    assign = (is0 | is1).astype(jnp.float32).astype(jnp.bfloat16)

    block = 48

    def norm(i, carry):
        rows = pl.ds(pl.multiple_of(i * block, 16), block)
        values = x_ref[rows, :].astype(jnp.float32)
        inverse = lax.rsqrt(jnp.mean(values * values, axis=-1, keepdims=True) + 1e-05)
        normed[rows, :] = (values * inverse * gain_ref[...]).astype(jnp.bfloat16)
        return carry

    inputs[1].wait()
    inputs[2].wait()
    with jax.named_scope("p_norm"):
        lax.fori_loop(0, tokens // block, norm, 0)

    piece = 512

    def fill(i, carry):
        part = pl.ds(pl.multiple_of(i * piece, piece), piece)
        send[:, part] = jnp.dot(
            assign, normed[:, part], preferred_element_type=jnp.float32
        ).astype(jnp.bfloat16)
        return carry

    with jax.named_scope("p_fill"):
        lax.fori_loop(0, width // piece, fill, 0)

    with jax.named_scope("p_barrier"):
        pl.semaphore_wait(barrier, PEERS + 2)

    def remote(src, dst, send_sem, recv_sem, target):
        return pltpu.make_async_remote_copy(
            src_ref=src, dst_ref=dst, send_sem=send_sem, recv_sem=recv_sem,
            device_id=target, device_id_type=MESH,
        )

    def rows_of(which):
        return pl.ds(pl.multiple_of(which * cap, cap), cap)

    def group_rows(g, skip=0):
        low, high = GROUPS[g]
        return pl.ds((low + skip) * cap, (high - low - skip) * cap)

    weights = ((up_ref, up_all), (down_ref, down_all))
    beside_copies = [
        remote(src, dst.at[pl.ds(2 * quarter, quarter)], xp_send.at[j], xp_recv.at[j], beside)
        for j, (src, dst) in enumerate(weights)
    ]
    sibling_copies = [
        remote(src, dst.at[pl.ds(quarter, quarter)], sib_send.at[j], sib_recv.at[j], sibling)
        for j, (src, dst) in enumerate(weights)
    ]
    for copy in beside_copies:
        copy.start()

    for g, (low, high) in enumerate(GROUPS):

        def go(i, carry, g=g):
            py, px = peer(i, 1)
            remote(
                send.at[rows_of(py * 2 + lax.div(px, 2))], recv.at[rows_of(i)],
                go_send.at[g], go_recv.at[g], device(py, px),
            ).start()
            return carry

        lax.fori_loop(max(low, 1), high, go, 0)
    stay = pltpu.make_async_copy(send.at[rows_of(mine)], recv.at[rows_of(0)], self_sem)
    stay.start()
    for copy in sibling_copies:
        copy.start()

    inputs[3].wait()
    gates = gates_ref[...]
    weight = jnp.where(is0, gates[0:1, :], 0.0) + jnp.where(is1, gates[1:2, :], 0.0)
    weight = weight.T
    high_part = weight.astype(jnp.bfloat16)
    mix[:, pl.ds(0, slots)] = high_part
    mix[:, pl.ds(slots, slots)] = (weight - high_part.astype(jnp.float32)).astype(jnp.bfloat16)

    forward_copies = [
        remote(
            dst.at[pl.ds(2 * quarter, quarter)], dst.at[pl.ds(3 * quarter, quarter)],
            fwd_send.at[j], fwd_recv.at[j], sibling,
        )
        for j, (_, dst) in enumerate(weights)
    ]
    for copy in own:
        copy.wait()
    for copy in sibling_copies:
        copy.wait()
    stay.wait()

    def went(g):
        rows = group_rows(g, 1 if g == 0 else 0)
        return remote(send.at[rows], recv.at[rows], go_send.at[g], go_recv.at[g], sibling)

    def home_copy(c, g):
        rows = group_rows(g, 1 if g == 0 else 0)
        return remote(res[c].at[rows], back[c].at[rows], home_send.at[c, g], home_recv.at[c, g], sibling)

    def keep(c):
        return pltpu.make_async_copy(res[c].at[rows_of(0)], back[c].at[rows_of(mine)], home_self.at[c])

    for j in range(2):
        with jax.named_scope(f"p_beside{j}"):
            beside_copies[j].wait_recv()
            forward_copies[j].start()
    units = 256
    for g, (low, high) in enumerate(GROUPS):
        rows = group_rows(g)
        with jax.named_scope("p_arrive"):
            went(g).wait_recv()
        if g == 0:
            with jax.named_scope("p_fwd0"):
                forward_copies[0].wait_recv()

        def up(i, carry, rows=rows):
            part = pl.ds(pl.multiple_of(i * units, units), units)
            v = lax.dot_general(
                recv[rows, :], up_all[part, :], (((1,), (1,)), ((), ())),
                preferred_element_type=jnp.float32,
            )
            inner = 0.7978845608028654 * (v + 0.044715 * (v * v * v))
            hidden[rows, part] = (0.5 * v * (1.0 + jnp.tanh(inner))).astype(jnp.bfloat16)
            return carry

        with jax.named_scope("p_up"):
            lax.fori_loop(0, 4 * quarter // units, up, 0)
        if g == 0:
            with jax.named_scope("p_fwd1"):
                forward_copies[1].wait_recv()
        for c in range(chunks):
            with jax.named_scope("p_down"):
                res[c][rows, :] = jnp.dot(
                    hidden[rows, :], down_all[:, pl.ds(STARTS[c], WIDTHS[c])],
                    preferred_element_type=jnp.float32,
                ).astype(jnp.bfloat16)

            def home(i, carry, c=c, g=g):
                py, px = peer(i, -1)
                remote(
                    res[c].at[rows_of(i)], back[c].at[rows_of(mine)],
                    home_send.at[c, g], home_recv.at[c, g], device(py, px),
                ).start()
                return carry

            with jax.named_scope("p_home"):
                lax.fori_loop(max(low, 1), high, home, 0)
            if g == 0:
                keep(c).start()

    onward = [
        remote(
            outb[c], out_ref.at[:, pl.ds(STARTS[c], WIDTHS[c])], out_send.at[c], out_recv.at[c], following
        )
        for c in range(chunks)
    ]
    for c in range(chunks):
        with jax.named_scope("p_came"):
            keep(c).wait()
            for g in range(len(GROUPS)):
                home_copy(c, g).wait_recv()
        with jax.named_scope("p_mix"):
            rows = back[c][...]
            total = jnp.dot(mix[:, pl.ds(0, slots)], rows, preferred_element_type=jnp.float32)
            total += jnp.dot(mix[:, pl.ds(slots, slots)], rows, preferred_element_type=jnp.float32)
            part = pl.ds(STARTS[c], WIDTHS[c])
            outb[c][...] = (x_ref[:, part].astype(jnp.float32) + total).astype(jnp.bfloat16)
            onward[c].start()

    for j in range(2):
        beside_copies[j].wait_send()
        forward_copies[j].wait_send()
    with jax.named_scope("p_drain"):
        for g in range(len(GROUPS)):
            went(g).wait_send()
            for c in range(chunks):
                home_copy(c, g).wait_send()
        for c in range(chunks):
            onward[c].wait()


def shards(carried, norm_gain, w_up, w_down, routes, gate_weights):
    tokens, width = carried.shape[1:]
    quarter = w_down.shape[1]
    slots = EXPERTS * 32
    bf16 = jnp.bfloat16
    dma = pltpu.SemaphoreType.DMA
    whole = pl.BlockSpec(memory_space=pl.ANY)
    chunks = len(WIDTHS)
    out = pl.pallas_call(
        kernel,
        name="section_layer",
        out_shape=jax.ShapeDtypeStruct((tokens, width), bf16),
        in_specs=[whole] * 6,
        out_specs=whole,
        scratch_shapes=[
            pltpu.VMEM((tokens, width), bf16),
            pltpu.VMEM((1, width), jnp.float32),
            pltpu.VMEM((2, tokens), jnp.int32),
            pltpu.VMEM((2, tokens), jnp.float32),
            pltpu.VMEM((4 * quarter, width), bf16),
            pltpu.VMEM((4 * quarter, width), bf16),
            pltpu.VMEM((tokens, width), bf16),
            pltpu.VMEM((slots, width), bf16),
            pltpu.VMEM((slots, width), bf16),
            pltpu.VMEM((slots, 4 * quarter), bf16),
            pltpu.VMEM((tokens, 2 * slots), bf16),
            *[pltpu.VMEM((slots, w), bf16) for w in WIDTHS],
            *[pltpu.VMEM((slots, w), bf16) for w in WIDTHS],
            *[pltpu.VMEM((tokens, w), bf16) for w in WIDTHS],
            dma((4,)), dma((2,)), dma((2,)), dma((2,)), dma((2,)), dma((2,)), dma((2,)), dma((2,)),
            dma, dma((len(GROUPS),)), dma((len(GROUPS),)),
            dma((chunks,)), dma((chunks, len(GROUPS))), dma((chunks, len(GROUPS))),
            dma((chunks,)), dma((chunks,)),
        ],
        compiler_params=pltpu.CompilerParams(
            collective_id=0, has_side_effects=True, vmem_limit_bytes=56 * 1024 * 1024
        ),
        cost_estimate=pl.CostEstimate(
            flops=16 * slots * width * quarter, bytes_accessed=8 * quarter * width, transcendentals=0
        ),
    )(carried[0], norm_gain, w_up[0].T, w_down[0], routes[0, 0].T, gate_weights[0, 0].T)
    return out[None]


def solution(mesh):
    in_specs = (
        P("section", "expert", None),
        P("section", None),
        P("section", None, "expert"),
        P("section", "expert", None),
        P(None, "section", "expert", None),
        P(None, "section", "expert", None),
    )
    return jax.shard_map(
        shards, mesh=mesh, in_specs=in_specs, out_specs=P("section", "expert", None), check_vma=False
    )
```

time: 141 us -> 126 us (0.89); the launches traced: 139 us -> 126 us
  Pallas kernels: 135 us -> 124 us
  local copies, waits for them, and re-layouts: 4.07 us -> 2.09 us
    pallas_call x1, Pallas kernels: 135 us -> 124 us  [shards(): pl.pallas_call(kernel, name='section_layer', out_shape=jax.ShapeDtypeStru...]
    unnamed x9 -> x1, local copies, waits for them, and re-layouts: 4.07 us -> 2.09 us
where the time goes in v2:
time: 126 us
  Pallas kernels  124 us (98%)
  local copies, waits for them, and re-layouts  2.09 us (2%)
    pallas_call x1, Pallas kernels, shards(): pl.pallas_call(kernel, name='section_layer', out_shape=jax.ShapeDtypeStru...  124 us

profile of v2, /device:TPU:1, one launch (start us, length us, event | category | flops | bytes accessed | tf_op | source)
XLA Modules:
  0.0 126.0 jit_solution(5222680866947322373)
XLA Ops:
  0.0 123.9 %section_layer.1 = bf16[192,2048]{1,0:T(8,128)(2,1)} custom-call(bf16[192,2048]{1,0:T(8,128)(2,1)} %bitcast.13, f32[1,2048]{1,0:T(1,128)} %gain_hbm.1, bf16[192,2048]{1,0:T(8,128)(2,1)} %bitcast.14, bf16[192,2048]{1,0:T(8,128)(2,1)} %bitcast.15, s32[2,192]{1,0:T(2,128)} %bitcast.16, f32[2,192]{1,0:T(2,128)} %bitcast.17), custom_call_target="tpu_custom_call" | custom-call | flops 3221225472 | bytes 3145728 | tf_op jit(solution)/shard_map/section_layer/pallas_call | solution.py:289
  123.9 2.1 %copy.8 = bf16[1,192,2048]{2,1,0:T(8,128)(2,1)} copy(bf16[1,192,2048]{2,1,0:T(8,128)(2,1)} %bitcast.12) | data formatting | bytes 1572864

commit v3 on v2

--- a/solution.py
+++ b/solution.py
@@ -10,20 +10,24 @@
 PEERS = 2 * NY
 EXPERTS = NX * NY // 2
 GROUPS = ((0, 10), (10, 16))
-WIDTHS = (640, 640, 512, 256)
+WIDTHS = (512, 512, 384)
+UNITS, UNIT = 5, 128
+DIRECT = 5
 STARTS = tuple(sum(WIDTHS[:c]) for c in range(len(WIDTHS)))
 
 
 def kernel(
     x_hbm, gain_hbm, up_ref, down_ref, routes_hbm, gates_hbm, out_ref,
     x_ref, gain_ref, routes_ref, gates_ref,
-    up_all, down_all, normed, send, recv, hidden, mix, *rest,
+    up_all, down_all, normed, send, recv, hidden, mix,
+    x_far, routes_far, gates_far, mix_far, res_unit, back_unit, out_unit, *rest,
 ):
     chunks = len(WIDTHS)
     res, back, outb = rest[:chunks], rest[chunks : 2 * chunks], rest[2 * chunks : 3 * chunks]
     (
         in_sem, own_sem, sib_send, sib_recv, xp_send, xp_recv, fwd_send, fwd_recv,
         self_sem, go_send, go_recv, home_self, home_send, home_recv, out_send, out_recv,
+        far_send, far_recv, unit_self, unit_send, unit_recv, unit_near, unit_far, unit_out_send, unit_out_recv, far_out, ready, late_ready,
     ) = rest[3 * chunks :]
     tokens, width = x_ref.shape
     quarter = up_ref.shape[0]
@@ -44,13 +48,25 @@
         dy = half * (2 * lax.rem(k, 2) - 1)
         return lax.rem(y + NY + sign * dy, NY), lax.rem(i, 2) * (NX - 1 - 2 * x) + x
 
-    def device(py, px):
-        return (section, (py * NX + px) * NC + core)
+    def device(py, px, where=section):
+        return (where, (py * NX + px) * NC + core)
 
     sibling = (section, chip * NC + 1 - core)
     beside = (section, (chip + 1 - 2 * lax.rem(x, 2)) * NC + core)
     following = (lax.rem(section + 1, sections), me)
     previous = (lax.rem(section + sections - 1, sections), me)
+    begin = STARTS[-1] + WIDTHS[-1]
+    passed = UNITS - lax.max(0, DIRECT - lax.rem(section + 1, sections))
+    taken = UNITS - lax.max(0, DIRECT - section)
+
+    last = sections - 1
+    kin = (core == 0) & ((x == 0) | (x == NX - 1))
+    is_late = (section == 0) & (me == 0)
+    near_late = (section == 0) & (me != 0) & (kin | (me == 1) | (me == NC))
+    next_late = (section == 1) & jnp.where(taken < UNITS, kin, me == 0)
+    punctual = jnp.logical_not(is_late)
+    onward_count = jnp.where(passed < UNITS, PEERS, 1)
+    before_count = jnp.where(taken < UNITS, PEERS, 1)
 
     def hello(target):
         pl.semaphore_signal(barrier, inc=1, device_id=target, device_id_type=MESH)
@@ -69,10 +85,30 @@
         hello(device(*peer(i, -1)))
         return carry
 
-    lax.fori_loop(1, PEERS, greet, 0)
-    hello(sibling)
-    hello(beside)
-    hello(previous)
+    def greet_at(where, number):
+        def greet_far(i, carry):
+            hello(device(*peer(i, -1), where))
+            return carry
+
+        lax.fori_loop(0, number, greet_far, 0)
+
+    @pl.when(punctual)
+    def _():
+        lax.fori_loop(1, PEERS, greet, 0)
+        hello(sibling)
+        hello(beside)
+
+    @pl.when(punctual & (section < last))
+    def _():
+        greet_at(section + 1, onward_count)
+
+    @pl.when(section == 0)
+    def _():
+        greet_at(last, before_count)
+
+    @pl.when(next_late)
+    def _():
+        hello((0, 0))
 
     own = [
         pltpu.make_async_copy(src, dst.at[pl.ds(0, quarter)], own_sem.at[j])
@@ -81,20 +117,35 @@
     for copy in own:
         copy.start()
 
+    def places(ids):
+        names = lax.broadcasted_iota(jnp.int32, (EXPERTS, tokens), 0)
+        first = (names == ids[0:1, :]).astype(jnp.float32)
+        second = (names == ids[1:2, :]).astype(jnp.float32)
+        earlier = (
+            lax.broadcasted_iota(jnp.int32, (tokens, tokens), 0)
+            < lax.broadcasted_iota(jnp.int32, (tokens, tokens), 1)
+        ).astype(jnp.bfloat16)
+        count = jnp.dot(
+            (first + second).astype(jnp.bfloat16), earlier, preferred_element_type=jnp.float32
+        )
+        place0 = jnp.sum(count * first, axis=0, keepdims=True).astype(jnp.int32) + ids[0:1, :] * cap
+        place1 = jnp.sum(count * second, axis=0, keepdims=True).astype(jnp.int32) + ids[1:2, :] * cap
+        slot = lax.broadcasted_iota(jnp.int32, (slots, tokens), 0)
+        return slot == place0, slot == place1
+
+    def fill_mix(mix, is0, is1, gates):
+        weight = jnp.where(is0, gates[0:1, :], 0.0) + jnp.where(is1, gates[1:2, :], 0.0)
+        weight = weight.T
+        high_part = weight.astype(jnp.bfloat16)
+        mix[:, pl.ds(0, slots)] = high_part
+        mix[:, pl.ds(slots, slots)] = (weight - high_part.astype(jnp.float32)).astype(jnp.bfloat16)
+
+    def mixed(mix, rows):
+        total = jnp.dot(mix[:, pl.ds(0, slots)], rows, preferred_element_type=jnp.float32)
+        return total + jnp.dot(mix[:, pl.ds(slots, slots)], rows, preferred_element_type=jnp.float32)
+
     inputs[0].wait()
-    ids = routes_ref[...]
-    names = lax.broadcasted_iota(jnp.int32, (EXPERTS, tokens), 0)
-    first = (names == ids[0:1, :]).astype(jnp.float32)
-    second = (names == ids[1:2, :]).astype(jnp.float32)
-    earlier = (
-        lax.broadcasted_iota(jnp.int32, (tokens, tokens), 0)
-        < lax.broadcasted_iota(jnp.int32, (tokens, tokens), 1)
-    ).astype(jnp.bfloat16)
-    count = jnp.dot((first + second).astype(jnp.bfloat16), earlier, preferred_element_type=jnp.float32)
-    place0 = jnp.sum(count * first, axis=0, keepdims=True).astype(jnp.int32) + ids[0:1, :] * cap
-    place1 = jnp.sum(count * second, axis=0, keepdims=True).astype(jnp.int32) + ids[1:2, :] * cap
-    slot = lax.broadcasted_iota(jnp.int32, (slots, tokens), 0)
-    is0, is1 = slot == place0, slot == place1
+    is0, is1 = places(routes_ref[...])
     assign = (is0 | is1).astype(jnp.float32).astype(jnp.bfloat16)
 
     block = 48
@@ -124,7 +175,14 @@
         lax.fori_loop(0, width // piece, fill, 0)
 
     with jax.named_scope("p_barrier"):
-        pl.semaphore_wait(barrier, PEERS + 2)
+        pl.semaphore_wait(
+            barrier,
+            PEERS + 1
+            - near_late.astype(jnp.int32)
+            + jnp.where(section > 0, before_count, 0)
+            - next_late.astype(jnp.int32)
+            + jnp.where((section == last) | is_late, onward_count, 0),
+        )
 
     def remote(src, dst, send_sem, recv_sem, target):
         return pltpu.make_async_remote_copy(
@@ -148,32 +206,98 @@
         remote(src, dst.at[pl.ds(quarter, quarter)], sib_send.at[j], sib_recv.at[j], sibling)
         for j, (src, dst) in enumerate(weights)
     ]
-    for copy in beside_copies:
-        copy.start()
-
-    for g, (low, high) in enumerate(GROUPS):
-
-        def go(i, carry, g=g):
-            py, px = peer(i, 1)
-            remote(
-                send.at[rows_of(py * 2 + lax.div(px, 2))], recv.at[rows_of(i)],
-                go_send.at[g], go_recv.at[g], device(py, px),
-            ).start()
-            return carry
-
-        lax.fori_loop(max(low, 1), high, go, 0)
+    @pl.when(is_late)
+    def _():
+        def arrived(target):
+            pl.semaphore_signal(late_ready, inc=1, device_id=target, device_id_type=MESH)
+
+        def tell_peer(i, carry):
+            arrived(device(*peer(i, 1)))
+            return carry
+
+        lax.fori_loop(1, PEERS, tell_peer, 0)
+        arrived(sibling)
+        arrived(beside)
+
+    def launch(copies, here):
+        @pl.when(here)
+        def _():
+            for copy in copies:
+                copy.start()
+
+    def go_all(late):
+        for g, (low, high) in enumerate(GROUPS):
+
+            def go(i, carry, g=g):
+                py, px = peer(i, 1)
+                target = device(py, px)
+                to_late = (section == 0) & (target[1] == 0)
+
+                @pl.when(to_late if late else jnp.logical_not(to_late))
+                def _():
+                    remote(
+                        send.at[rows_of(py * 2 + lax.div(px, 2))], recv.at[rows_of(i)],
+                        go_send.at[g], go_recv.at[g], target,
+                    ).start()
+
+                return carry
+
+            lax.fori_loop(max(low, 1), high, go, 0)
+
+    beside_late = (section == 0) & (me == NC)
+    sibling_late = (section == 0) & (me == 1)
+    launch(beside_copies, jnp.logical_not(beside_late))
+    go_all(False)
     stay = pltpu.make_async_copy(send.at[rows_of(mine)], recv.at[rows_of(0)], self_sem)
     stay.start()
-    for copy in sibling_copies:
-        copy.start()
-
+
+    @pl.when(section > 0)
+    def _():
+        def tell(i, carry):
+            target = device(*peer(i, 1), section - 1)
+
+            @pl.when(jnp.logical_not((section == 1) & (target[1] == 0)))
+            def _():
+                pl.semaphore_signal(ready, inc=1, device_id=target, device_id_type=MESH)
+
+            return carry
+
+        lax.fori_loop(0, before_count, tell, 0)
+
+    launch(sibling_copies, jnp.logical_not(sibling_late))
     inputs[3].wait()
-    gates = gates_ref[...]
-    weight = jnp.where(is0, gates[0:1, :], 0.0) + jnp.where(is1, gates[1:2, :], 0.0)
-    weight = weight.T
-    high_part = weight.astype(jnp.bfloat16)
-    mix[:, pl.ds(0, slots)] = high_part
-    mix[:, pl.ds(slots, slots)] = (weight - high_part.astype(jnp.float32)).astype(jnp.bfloat16)
+    far_copies = [
+        remote(src, dst, far_send.at[j], far_recv.at[j], following)
+        for j, (src, dst) in enumerate(
+            (
+                (routes_ref, routes_far),
+                (gates_ref, gates_far),
+                (x_ref.at[:, pl.ds(begin, UNITS * UNIT)], x_far),
+            )
+        )
+    ]
+
+    fill_mix(mix, is0, is1, gates_ref[...])
+
+    @pl.when(punctual & (section < last))
+    def _():
+        pl.semaphore_wait(ready, onward_count)
+
+    @pl.when(passed < UNITS)
+    def _():
+        for copy in far_copies:
+            copy.start()
+
+    @pl.when(near_late)
+    def _():
+        pl.semaphore_wait(late_ready, 1)
+
+    @pl.when(near_late & kin)
+    def _():
+        go_all(True)
+
+    launch(beside_copies, beside_late)
+    launch(sibling_copies, sibling_late)
 
     forward_copies = [
         remote(
@@ -246,6 +370,69 @@
                 lax.fori_loop(max(low, 1), high, home, 0)
             if g == 0:
                 keep(c).start()
+        tail = jnp.dot(
+            hidden[rows, :], down_all[:, pl.ds(begin, UNITS * UNIT)], preferred_element_type=jnp.float32
+        ).astype(jnp.bfloat16)
+        for j in range(UNITS):
+            res_unit[j, rows, :] = tail[:, j * UNIT : (j + 1) * UNIT]
+
+    def unit_wait(d, j, g):
+        rows = group_rows(g, 1 if g == 0 else 0)
+        return remote(
+            res_unit.at[j, rows], back_unit.at[d, j, rows],
+            unit_send.at[j, g], unit_recv.at[d, j, g], sibling,
+        )
+
+    def unit_keep(j):
+        return pltpu.make_async_copy(
+            res_unit.at[j, rows_of(0)], back_unit.at[0, j, rows_of(mine)], unit_self.at[j]
+        )
+
+    def unit_hand(j):
+        return remote(
+            res_unit.at[j, rows_of(0)], back_unit.at[1, j, rows_of(mine)],
+            unit_near.at[j], unit_far.at[j], following,
+        )
+
+    def unit_columns(j):
+        return pl.ds(pl.multiple_of(begin + j * UNIT, UNIT), UNIT)
+
+    def unit_onward(j):
+        return remote(
+            out_unit.at[j], out_ref.at[:, unit_columns(j)],
+            unit_out_send.at[j], unit_out_recv.at[j], following,
+        )
+
+    def unit_store(j):
+        return pltpu.make_async_copy(out_unit.at[UNITS + j], out_ref.at[:, unit_columns(j)], far_out.at[j])
+
+    def unit_home(j, carry):
+        d = (j >= passed).astype(jnp.int32)
+        where = lax.rem(section + d, sections)
+        for g, (low, high) in enumerate(GROUPS):
+
+            def home(i, inner, g=g):
+                py, px = peer(i, -1)
+                remote(
+                    res_unit.at[j, rows_of(i)], back_unit.at[d, j, rows_of(mine)],
+                    unit_send.at[j, g], unit_recv.at[d, j, g], device(py, px, where),
+                ).start()
+                return inner
+
+            lax.fori_loop(max(low, 1), high, home, 0)
+
+        @pl.when(j < passed)
+        def _():
+            unit_keep(j).start()
+
+        @pl.when(j >= passed)
+        def _():
+            unit_hand(j).start()
+
+        return carry
+
+    with jax.named_scope("p_unithome"):
+        lax.fori_loop(0, UNITS, unit_home, 0)
 
     onward = [
         remote(
@@ -259,12 +446,40 @@
             for g in range(len(GROUPS)):
                 home_copy(c, g).wait_recv()
         with jax.named_scope("p_mix"):
-            rows = back[c][...]
-            total = jnp.dot(mix[:, pl.ds(0, slots)], rows, preferred_element_type=jnp.float32)
-            total += jnp.dot(mix[:, pl.ds(slots, slots)], rows, preferred_element_type=jnp.float32)
             part = pl.ds(STARTS[c], WIDTHS[c])
-            outb[c][...] = (x_ref[:, part].astype(jnp.float32) + total).astype(jnp.bfloat16)
+            total = x_ref[:, part].astype(jnp.float32) + mixed(mix, back[c][...])
+            outb[c][...] = total.astype(jnp.bfloat16)
             onward[c].start()
+
+    def unit_finish(j, carry):
+        unit_keep(j).wait()
+        for g in range(len(GROUPS)):
+            unit_wait(0, j, g).wait_recv()
+        total = x_ref[:, unit_columns(j)].astype(jnp.float32) + mixed(mix, back_unit[0, j])
+        out_unit[j] = total.astype(jnp.bfloat16)
+        unit_onward(j).start()
+        return carry
+
+    def unit_finish_far(j, carry):
+        unit_hand(j).wait_recv()
+        for g in range(len(GROUPS)):
+            unit_wait(1, j, g).wait_recv()
+        part = pl.ds(pl.multiple_of(j * UNIT, UNIT), UNIT)
+        total = x_far[:, part].astype(jnp.float32) + mixed(mix_far, back_unit[1, j])
+        out_unit[UNITS + j] = total.astype(jnp.bfloat16)
+        unit_store(j).start()
+        return carry
+
+    with jax.named_scope("p_unitfin"):
+        lax.fori_loop(0, passed, unit_finish, 0)
+    @pl.when(taken < UNITS)
+    def _():
+        for copy in far_copies:
+            copy.wait_recv()
+        fill_mix(mix_far, *places(routes_far[...]), gates_far[...])
+
+    with jax.named_scope("p_unitfar"):
+        lax.fori_loop(taken, UNITS, unit_finish_far, 0)
 
     for j in range(2):
         beside_copies[j].wait_send()
@@ -276,6 +491,38 @@
                 home_copy(c, g).wait_send()
         for c in range(chunks):
             onward[c].wait()
+
+        def drain_sent(j, carry):
+            for g in range(len(GROUPS)):
+                unit_wait(0, j, g).wait_send()
+            return carry
+
+        def drain_onward(j, carry):
+            unit_onward(j).wait_send()
+            return carry
+
+        def drain_hand(j, carry):
+            unit_hand(j).wait_send()
+            return carry
+
+        def drain_came(j, carry):
+            unit_onward(j).wait_recv()
+            return carry
+
+        def drain_store(j, carry):
+            unit_store(j).wait()
+            return carry
+
+        lax.fori_loop(0, UNITS, drain_sent, 0)
+        lax.fori_loop(0, passed, drain_onward, 0)
+        lax.fori_loop(passed, UNITS, drain_hand, 0)
+        lax.fori_loop(0, taken, drain_came, 0)
+        lax.fori_loop(taken, UNITS, drain_store, 0)
+
+        @pl.when(passed < UNITS)
+        def _():
+            for copy in far_copies:
+                copy.wait_send()
 
 
 def shards(carried, norm_gain, w_up, w_down, routes, gate_weights):
@@ -304,6 +551,13 @@
             pltpu.VMEM((slots, width), bf16),
             pltpu.VMEM((slots, 4 * quarter), bf16),
             pltpu.VMEM((tokens, 2 * slots), bf16),
+            pltpu.VMEM((tokens, UNITS * UNIT), bf16),
+            pltpu.VMEM((2, tokens), jnp.int32),
+            pltpu.VMEM((2, tokens), jnp.float32),
+            pltpu.VMEM((tokens, 2 * slots), bf16),
+            pltpu.VMEM((UNITS, slots, UNIT), bf16),
+            pltpu.VMEM((2, UNITS, slots, UNIT), bf16),
+            pltpu.VMEM((2 * UNITS, tokens, UNIT), bf16),
             *[pltpu.VMEM((slots, w), bf16) for w in WIDTHS],
             *[pltpu.VMEM((slots, w), bf16) for w in WIDTHS],
             *[pltpu.VMEM((tokens, w), bf16) for w in WIDTHS],
@@ -311,6 +565,9 @@
             dma, dma((len(GROUPS),)), dma((len(GROUPS),)),
             dma((chunks,)), dma((chunks, len(GROUPS))), dma((chunks, len(GROUPS))),
             dma((chunks,)), dma((chunks,)),
+            dma((3,)), dma((3,)), dma((UNITS,)), dma((UNITS, len(GROUPS))), dma((2, UNITS, len(GROUPS))),
+            dma((UNITS,)), dma((UNITS,)), dma((UNITS,)), dma((UNITS,)), dma((UNITS,)),
+            pltpu.SemaphoreType.REGULAR, pltpu.SemaphoreType.REGULAR,
         ],
         compiler_params=pltpu.CompilerParams(
             collective_id=0, has_side_effects=True, vmem_limit_bytes=56 * 1024 * 1024

time: 126 us -> 114 us (0.905); the launches traced: 126 us -> 112 us
  Pallas kernels: 124 us -> 110 us
    pallas_call x1, Pallas kernels: 124 us -> 110 us  [shards(): pl.pallas_call(kernel, name='section_layer', out_shape=jax.ShapeDtypeStru...]
where the time goes in v3:
time: 114 us; the launch traced here: 112 us
  Pallas kernels  110 us (96%)
  local copies, waits for them, and re-layouts  2.09 us (2%)
    pallas_call x1, Pallas kernels, shards(): pl.pallas_call(kernel, name='section_layer', out_shape=jax.ShapeDtypeStru...  110 us

profile of v3, /device:TPU:1, one launch (start us, length us, event | category | flops | bytes accessed | tf_op | source)
XLA Modules:
  0.0 112.4 jit_solution(6157742960429413778)
XLA Ops:
  0.0 110.3 %section_layer.1 = bf16[192,2048]{1,0:T(8,128)(2,1)} custom-call(bf16[192,2048]{1,0:T(8,128)(2,1)} %bitcast.13, f32[1,2048]{1,0:T(1,128)} %gain_hbm.1, bf16[192,2048]{1,0:T(8,128)(2,1)} %bitcast.14, bf16[192,2048]{1,0:T(8,128)(2,1)} %bitcast.15, s32[2,192]{1,0:T(2,128)} %bitcast.16, f32[2,192]{1,0:T(2,128)} %bitcast.17), custom_call_target="tpu_custom_call" | custom-call | flops 3221225472 | bytes 3145728 | tf_op jit(solution)/shard_map/section_layer/pallas_call | solution.py:536
  110.3 2.1 %copy.8 = bf16[1,192,2048]{2,1,0:T(8,128)(2,1)} copy(bf16[1,192,2048]{2,1,0:T(8,128)(2,1)} %bitcast.12) | data formatting | bytes 1572864

commit v4 on v3

--- a/solution.py
+++ b/solution.py
@@ -10,9 +10,9 @@
 PEERS = 2 * NY
 EXPERTS = NX * NY // 2
 GROUPS = ((0, 10), (10, 16))
-WIDTHS = (512, 512, 384)
+WIDTHS = (512, 512, 256, 128)
 UNITS, UNIT = 5, 128
-DIRECT = 5
+DIRECT = 6
 STARTS = tuple(sum(WIDTHS[:c]) for c in range(len(WIDTHS)))
 
 
@@ -20,14 +20,14 @@
     x_hbm, gain_hbm, up_ref, down_ref, routes_hbm, gates_hbm, out_ref,
     x_ref, gain_ref, routes_ref, gates_ref,
     up_all, down_all, normed, send, recv, hidden, mix,
-    x_far, routes_far, gates_far, mix_far, res_unit, back_unit, out_unit, *rest,
+    x_far, routes_far, gates_far, mix_far, res_unit, back_unit, out_unit, relay, *rest,
 ):
     chunks = len(WIDTHS)
     res, back, outb = rest[:chunks], rest[chunks : 2 * chunks], rest[2 * chunks : 3 * chunks]
     (
         in_sem, own_sem, sib_send, sib_recv, xp_send, xp_recv, fwd_send, fwd_recv,
         self_sem, go_send, go_recv, home_self, home_send, home_recv, out_send, out_recv,
-        far_send, far_recv, unit_self, unit_send, unit_recv, unit_near, unit_far, unit_out_send, unit_out_recv, far_out, ready, late_ready,
+        far_send, far_recv, unit_self, unit_send, unit_recv, unit_near, unit_far, unit_out_send, unit_out_recv, far_out, ready, late_ready, relay_send, relay_recv,
     ) = rest[3 * chunks :]
     tokens, width = x_ref.shape
     quarter = up_ref.shape[0]
@@ -56,12 +56,14 @@
     following = (lax.rem(section + 1, sections), me)
     previous = (lax.rem(section + sections - 1, sections), me)
     begin = STARTS[-1] + WIDTHS[-1]
-    passed = UNITS - lax.max(0, DIRECT - lax.rem(section + 1, sections))
-    taken = UNITS - lax.max(0, DIRECT - section)
+    passed = UNITS - lax.min(UNITS, lax.max(0, DIRECT - lax.rem(section + 1, sections)))
+    taken = UNITS - lax.min(UNITS, lax.max(0, DIRECT - section))
 
     last = sections - 1
     kin = (core == 0) & ((x == 0) | (x == NX - 1))
     is_late = (section == 0) & (me == 0)
+    sibling_late = (section == 0) & (me == 1)
+    beside_late = (section == 0) & (me == NC)
     near_late = (section == 0) & (me != 0) & (kin | (me == 1) | (me == NC))
     next_late = (section == 1) & jnp.where(taken < UNITS, kin, me == 0)
     punctual = jnp.logical_not(is_late)
@@ -82,7 +84,7 @@
         copy.start()
 
     def greet(i, carry):
-        hello(device(*peer(i, -1)))
+        hello(device(*peer(PEERS - i, -1)))
         return carry
 
     def greet_at(where, number):
@@ -109,6 +111,15 @@
     @pl.when(next_late)
     def _():
         hello((0, 0))
+
+    @pl.when(sibling_late)
+    def _():
+        def greet_for(i, carry):
+            py, px = peer(i, -1)
+            hello((section, (py * NX + px) * NC))
+            return carry
+
+        lax.fori_loop(1, PEERS, greet_for, 0)
 
     own = [
         pltpu.make_async_copy(src, dst.at[pl.ds(0, quarter)], own_sem.at[j])
@@ -178,7 +189,7 @@
         pl.semaphore_wait(
             barrier,
             PEERS + 1
-            - near_late.astype(jnp.int32)
+            - (sibling_late | beside_late).astype(jnp.int32)
             + jnp.where(section > 0, before_count, 0)
             - next_late.astype(jnp.int32)
             + jnp.where((section == last) | is_late, onward_count, 0),
@@ -225,29 +236,27 @@
             for copy in copies:
                 copy.start()
 
-    def go_all(late):
-        for g, (low, high) in enumerate(GROUPS):
-
-            def go(i, carry, g=g):
-                py, px = peer(i, 1)
-                target = device(py, px)
-                to_late = (section == 0) & (target[1] == 0)
-
-                @pl.when(to_late if late else jnp.logical_not(to_late))
-                def _():
-                    remote(
-                        send.at[rows_of(py * 2 + lax.div(px, 2))], recv.at[rows_of(i)],
-                        go_send.at[g], go_recv.at[g], target,
-                    ).start()
-
-                return carry
-
-            lax.fori_loop(max(low, 1), high, go, 0)
-
-    beside_late = (section == 0) & (me == NC)
-    sibling_late = (section == 0) & (me == 1)
     launch(beside_copies, jnp.logical_not(beside_late))
-    go_all(False)
+    for g, (low, high) in enumerate(GROUPS):
+
+        def go(i, carry, g=g):
+            py, px = peer(i, 1)
+            target = device(py, px)
+            source = send.at[rows_of(py * 2 + lax.div(px, 2))]
+            to_late = (section == 0) & (target[1] == 0)
+
+            @pl.when(jnp.logical_not(to_late))
+            def _():
+                remote(source, recv.at[rows_of(i)], go_send.at[g], go_recv.at[g], target).start()
+
+            @pl.when(to_late)
+            def _():
+                remote(source, relay.at[rows_of(i)], go_send.at[g], relay_recv.at[g], (section, 1)).start()
+
+            return carry
+
+        lax.fori_loop(max(low, 1), high, go, 0)
+
     stay = pltpu.make_async_copy(send.at[rows_of(mine)], recv.at[rows_of(0)], self_sem)
     stay.start()
 
@@ -292,10 +301,6 @@
     def _():
         pl.semaphore_wait(late_ready, 1)
 
-    @pl.when(near_late & kin)
-    def _():
-        go_all(True)
-
     launch(beside_copies, beside_late)
     launch(sibling_copies, sibling_late)
 
@@ -322,6 +327,14 @@
 
     def keep(c):
         return pltpu.make_async_copy(res[c].at[rows_of(0)], back[c].at[rows_of(mine)], home_self.at[c])
+
+    def passing(g):
+        rows = group_rows(g, 1 if g == 0 else 0)
+        return remote(relay.at[rows], recv.at[rows], relay_send.at[g], go_recv.at[g], sibling)
+
+    def came_to_pass(g):
+        rows = group_rows(g, 1 if g == 0 else 0)
+        return remote(send.at[rows], relay.at[rows], go_send.at[g], relay_recv.at[g], sibling)
 
     for j in range(2):
         with jax.named_scope(f"p_beside{j}"):
@@ -332,6 +345,12 @@
         rows = group_rows(g)
         with jax.named_scope("p_arrive"):
             went(g).wait_recv()
+
+        @pl.when(sibling_late)
+        def _(g=g):
+            came_to_pass(g).wait_recv()
+            passing(g).start()
+
         if g == 0:
             with jax.named_scope("p_fwd0"):
                 forward_copies[0].wait_recv()
@@ -487,6 +506,11 @@
     with jax.named_scope("p_drain"):
         for g in range(len(GROUPS)):
             went(g).wait_send()
+
+            @pl.when(sibling_late)
+            def _(g=g):
+                passing(g).wait_send()
+
             for c in range(chunks):
                 home_copy(c, g).wait_send()
         for c in range(chunks):
@@ -558,6 +582,7 @@
             pltpu.VMEM((UNITS, slots, UNIT), bf16),
             pltpu.VMEM((2, UNITS, slots, UNIT), bf16),
             pltpu.VMEM((2 * UNITS, tokens, UNIT), bf16),
+            pltpu.VMEM((slots, width), bf16),
             *[pltpu.VMEM((slots, w), bf16) for w in WIDTHS],
             *[pltpu.VMEM((slots, w), bf16) for w in WIDTHS],
             *[pltpu.VMEM((tokens, w), bf16) for w in WIDTHS],
@@ -567,7 +592,7 @@
             dma((chunks,)), dma((chunks,)),
             dma((3,)), dma((3,)), dma((UNITS,)), dma((UNITS, len(GROUPS))), dma((2, UNITS, len(GROUPS))),
             dma((UNITS,)), dma((UNITS,)), dma((UNITS,)), dma((UNITS,)), dma((UNITS,)),
-            pltpu.SemaphoreType.REGULAR, pltpu.SemaphoreType.REGULAR,
+            pltpu.SemaphoreType.REGULAR, pltpu.SemaphoreType.REGULAR, dma((len(GROUPS),)), dma((len(GROUPS),)),
         ],
         compiler_params=pltpu.CompilerParams(
             collective_id=0, has_side_effects=True, vmem_limit_bytes=56 * 1024 * 1024

time: 114 us -> 113 us (level)
    pallas_call x1, Pallas kernels: 110 us -> 109 us  [shards(): pl.pallas_call(kernel, name='section_layer', out_shape=jax.ShapeDtypeStru...]
where the time goes in v4:
time: 113 us; the launch traced here: 111 us
  Pallas kernels  109 us (96%)
  local copies, waits for them, and re-layouts  2.09 us (2%)
    pallas_call x1, Pallas kernels, shards(): pl.pallas_call(kernel, name='section_layer', out_shape=jax.ShapeDtypeStru...  109 us

profile of v4, /device:TPU:1, one launch (start us, length us, event | category | flops | bytes accessed | tf_op | source)
XLA Modules:
  0.0 110.6 jit_solution(8398619223129920538)
XLA Ops:
  0.0 108.5 %section_layer.1 = bf16[192,2048]{1,0:T(8,128)(2,1)} custom-call(bf16[192,2048]{1,0:T(8,128)(2,1)} %bitcast.13, f32[1,2048]{1,0:T(1,128)} %gain_hbm.1, bf16[192,2048]{1,0:T(8,128)(2,1)} %bitcast.14, bf16[192,2048]{1,0:T(8,128)(2,1)} %bitcast.15, s32[2,192]{1,0:T(2,128)} %bitcast.16, f32[2,192]{1,0:T(2,128)} %bitcast.17), custom_call_target="tpu_custom_call" | custom-call | flops 3221225472 | bytes 3145728 | tf_op jit(solution)/shard_map/section_layer/pallas_call | solution.py:560
  108.5 2.1 %copy.8 = bf16[1,192,2048]{2,1,0:T(8,128)(2,1)} copy(bf16[1,192,2048]{2,1,0:T(8,128)(2,1)} %bitcast.12) | data formatting | bytes 1572864

commit v5 on v4

--- a/solution.py
+++ b/solution.py
@@ -10,7 +10,7 @@
 PEERS = 2 * NY
 EXPERTS = NX * NY // 2
 GROUPS = ((0, 10), (10, 16))
-WIDTHS = (512, 512, 256, 128)
+WIDTHS = (384, 384, 256, 256, 128)
 UNITS, UNIT = 5, 128
 DIRECT = 6
 STARTS = tuple(sum(WIDTHS[:c]) for c in range(len(WIDTHS)))

time: 113 us -> 112 us (level)
  no operation moved by 1% of the time
where the time goes in v5:
time: 112 us; the launch traced here: 110 us
  Pallas kernels  108 us (96%)
  local copies, waits for them, and re-layouts  2.09 us (2%)
    pallas_call x1, Pallas kernels, shards(): pl.pallas_call(kernel, name='section_layer', out_shape=jax.ShapeDtypeStru...  108 us

profile of v5, /device:TPU:1, one launch (start us, length us, event | category | flops | bytes accessed | tf_op | source)
XLA Modules:
  0.0 110.4 jit_solution(11223862913025856497)
XLA Ops:
  0.0 108.3 %section_layer.1 = bf16[192,2048]{1,0:T(8,128)(2,1)} custom-call(bf16[192,2048]{1,0:T(8,128)(2,1)} %bitcast.13, f32[1,2048]{1,0:T(1,128)} %gain_hbm.1, bf16[192,2048]{1,0:T(8,128)(2,1)} %bitcast.14, bf16[192,2048]{1,0:T(8,128)(2,1)} %bitcast.15, s32[2,192]{1,0:T(2,128)} %bitcast.16, f32[2,192]{1,0:T(2,128)} %bitcast.17), custom_call_target="tpu_custom_call" | custom-call | flops 3221225472 | bytes 3145728 | tf_op jit(solution)/shard_map/section_layer/pallas_call | solution.py:560
  108.4 2.1 %copy.8 = bf16[1,192,2048]{2,1,0:T(8,128)(2,1)} copy(bf16[1,192,2048]{2,1,0:T(8,128)(2,1)} %bitcast.12) | data formatting | bytes 1572864

commit v6 on v5

--- a/solution.py
+++ b/solution.py
@@ -9,7 +9,7 @@
 NX, NY, NC = 4, 8, 2
 PEERS = 2 * NY
 EXPERTS = NX * NY // 2
-GROUPS = ((0, 10), (10, 16))
+GROUPS = ((0, 8), (8, 16))
 WIDTHS = (384, 384, 256, 256, 128)
 UNITS, UNIT = 5, 128
 DIRECT = 6

time: 112 us -> 112 us (level)
  the two profiles are of different devices: /device:TPU:1 before, /device:TPU:6 now
where the time goes in v6:
time: 112 us; the launch traced here: 111 us
  Pallas kernels  109 us (97%)
  local copies, waits for them, and re-layouts  2.09 us (2%)
    pallas_call x1, Pallas kernels, shards(): pl.pallas_call(kernel, name='section_layer', out_shape=jax.ShapeDtypeStru...  109 us

profile of v6, /device:TPU:6, one launch (start us, length us, event | category | flops | bytes accessed | tf_op | source)
XLA Modules:
  0.0 111.4 jit_solution(15381802390741829518)
XLA Ops:
  0.0 109.3 %section_layer.1 = bf16[192,2048]{1,0:T(8,128)(2,1)} custom-call(bf16[192,2048]{1,0:T(8,128)(2,1)} %bitcast.13, f32[1,2048]{1,0:T(1,128)} %gain_hbm.1, bf16[192,2048]{1,0:T(8,128)(2,1)} %bitcast.14, bf16[192,2048]{1,0:T(8,128)(2,1)} %bitcast.15, s32[2,192]{1,0:T(2,128)} %bitcast.16, f32[2,192]{1,0:T(2,128)} %bitcast.17), custom_call_target="tpu_custom_call" | custom-call | flops 3221225472 | bytes 3145728 | tf_op jit(solution)/shard_map/section_layer/pallas_call | solution.py:560
  109.3 2.1 %copy.8 = bf16[1,192,2048]{2,1,0:T(8,128)(2,1)} copy(bf16[1,192,2048]{2,1,0:T(8,128)(2,1)} %bitcast.12) | data formatting | bytes 1572864
